TPU v7x, 32 devices: a whole 2x2x4 slice. The times are simulated.
32 devices in a mesh: blocks: 8 (over z, x), rep: 4 (over y, core).
Axes of the slice: x: 2, y: 2, z: 4, core: 2. Of those that a mesh axis runs over, the one named last changes fastest.
Arguments:
- features: bfloat16 [4, 32, 512, 128], P('rep', 'blocks'), may hold values from -6 to 6
- weight_one: bfloat16 [27, 128, 128], replicated, may hold values from -0.109375 to 0.109375
- weight_two: bfloat16 [27, 128, 128], replicated, may hold values from -0.109375 to 0.109375
- cotangent: bfloat16 [4, 32, 512, 128], P('rep', 'blocks'), may hold values from -6 to 6
- neighbours: int32 [4, 32, 26], P('rep', 'blocks'), may hold values from -1 to 31, as said below
Outputs:
- segment_out: bfloat16 [4, 32, 512, 128], P('rep', 'blocks')
- grad_one: float32 [27, 128, 128], replicated
- grad_two: float32 [27, 128, 128], replicated
Inputs may be any that keep to these rules, and one draw needn't show every extreme that they name: neighbours[s, b, k] is the active block at offset k from block b in the slab of scene s, or -1 where that block is empty or outside the slab; blocks are ordered by x, then within each cross-section of 4 x 4 blocks by the Morton alternate of y and z, taken in reverse on odd x; block b belongs to device b // 4 of the axis blocks; the relation is symmetric (b names n at an offset exactly when n names b at the opposite one); the devices of a block and of any of its neighbours differ by at most 7 in index, and in every scene some pair differs by exactly 7.
All inputs are finite; a program needn't handle non-finite values.
Results may differ from a plain program's by a relative error of at most 0.005.
Values may be sent and summed in bfloat16 or wider, within the bound.
A program may use at most 128 MiB of HBM per device.

v0:
```python
import functools
import math

import jax
import jax.numpy as jnp
from jax import lax
from jax.experimental import pallas as pl
from jax.experimental.pallas import tpu as pltpu
from jax.sharding import PartitionSpec as P

VMEM_LIMIT = 56 * 1024 * 1024


def offset_index(step_x, step_y, step_z):
    place = 9 * (step_x + 1) + 3 * (step_y + 1) + (step_z + 1)
    return place if place < 13 else place - 1


def from_behind(block, axis, distance):
    devices = range(lax.axis_size(axis))
    route = [(i - distance, i) for i in devices if i - distance in devices]
    return lax.ppermute(block, axis, route)


def lines_of(rows):
    return rows.astype(jnp.float32).reshape(-1, 8, rows.shape[-1])


def build_slab(block, own_ref, table_ref, place_ref, pad_ref, slab_ref):
    channels = own_ref.shape[-1]

    def place(step_x, step_y, step_z):
        return place_ref[block, offset_index(step_x, step_y, step_z)]

    def source(step_x, step_y, step_z, plane, rows):
        if (step_x, step_y, step_z) == (0, 0, 0):
            return lines_of(own_ref[block, plane, rows, :])
        where = place(step_x, step_y, step_z)
        got = lines_of(table_ref[jnp.maximum(where, 0), plane, rows, :])
        return jnp.where(where >= 0, got, 0.0)

    def put(ii, first_line, step_x, step_y, plane, rows, pick):
        mid, low, high = (
            source(step_x, step_y, step_z, plane, rows)[pick] for step_z in (0, -1, 1)
        )
        cell = lax.broadcasted_iota(jnp.int32, mid.shape, 1)
        count = mid.shape[0]
        shifted = (
            pltpu.roll(jnp.where(cell == 7, low, mid), 1, 1),
            mid,
            pltpu.roll(jnp.where(cell == 0, high, mid), 7, 1),
        )
        for tap_c in range(3):
            pad_ref[tap_c, ii, pl.ds(8 * first_line, 8 * count), :] = shifted[tap_c].reshape(
                8 * count, channels
            )

    every = slice(None)
    for ii in range(10):
        step_x = -1 if ii == 0 else (1 if ii == 9 else 0)
        plane = 7 if ii == 0 else (0 if ii == 9 else ii - 1)
        put(ii, 0, step_x, -1, plane, slice(48, 64), slice(1, 2))
        put(ii, 1, step_x, 0, plane, slice(0, 64), every)
        put(ii, 9, step_x, 1, plane, slice(0, 16), slice(0, 1))
    for tap_b in range(3):
        for tap_c in range(3):
            column = (3 * tap_b + tap_c) * channels
            slab_ref[:, pl.ds(column, channels)] = (
                pad_ref[tap_c, :, pl.ds(8 * tap_b, 64), :]
                .reshape(640, channels)
                .astype(jnp.bfloat16)
            )


def conv_slab(slab_ref, weight_ref):
    total = None
    for tap_a in range(3):
        part = jnp.dot(
            slab_ref[pl.ds(64 * tap_a, 512), :],
            weight_ref[tap_a],
            preferred_element_type=jnp.float32,
        )
        total = part if total is None else total + part
    return total


def spread_rows(spread_ref, rows):
    channels = rows.shape[-1]
    spread_ref[...] = jnp.zeros_like(spread_ref)
    for tap_a in range(3):
        spread_ref[pl.ds(64 * tap_a, 512), pl.ds(tap_a * channels, channels)] = rows


def add_taps(total_ref, spread_ref, slab_ref):
    total_ref[...] += jnp.dot(
        spread_ref[...].T, slab_ref[...], preferred_element_type=jnp.float32
    )


def write_taps(total_ref, grad_ref, scale):
    channels = grad_ref.shape[-1]
    for tap_a in range(3):
        for tap_bc in range(9):
            piece = total_ref[
                pl.ds(tap_a * channels, channels), pl.ds(tap_bc * channels, channels)
            ]
            grad_ref[9 * tap_a + tap_bc] = piece.T * scale


def sigmoid(values):
    return 1.0 / (1.0 + jnp.exp(-values))


def first_kernel(place_ref, own_ref, table_ref, weight_ref, pre_ref, hidden_ref, pad_ref, slab_ref):
    def step(block, carry):
        build_slab(block, own_ref, table_ref, place_ref, pad_ref, slab_ref)
        pre = conv_slab(slab_ref, weight_ref)
        pre_ref[block] = pre
        hidden_ref[block] = (pre / (1.0 + jnp.exp(-pre))).astype(jnp.bfloat16)
        return carry

    lax.fori_loop(0, own_ref.shape[0], step, 0)


def back_kernel(
    scale, place_ref, own_ref, table_ref, cot_ref, cot_table_ref, weight_ref, pre_ref,
    grad_ref, pad_ref, slab_ref, spread_ref, total_ref,
):
    total_ref[...] = jnp.zeros_like(total_ref)

    def step(block, carry):
        build_slab(block, cot_ref, cot_table_ref, place_ref, pad_ref, slab_ref)
        back = conv_slab(slab_ref, weight_ref)
        pre = pre_ref[block]
        sig = sigmoid(pre)
        delta = (back * (sig * (1.0 + pre * (1.0 - sig)))).astype(jnp.bfloat16)
        spread_rows(spread_ref, delta)
        build_slab(block, own_ref, table_ref, place_ref, pad_ref, slab_ref)
        add_taps(total_ref, spread_ref, slab_ref)
        return carry

    lax.fori_loop(0, own_ref.shape[0], step, 0)
    write_taps(total_ref, grad_ref, scale)


def second_kernel(
    scale, place_ref, own_ref, table_ref, cot_ref, weight_ref,
    out_ref, grad_ref, pad_ref, slab_ref, spread_ref, total_ref,
):
    total_ref[...] = jnp.zeros_like(total_ref)

    def step(block, carry):
        build_slab(block, own_ref, table_ref, place_ref, pad_ref, slab_ref)
        out_ref[block] = conv_slab(slab_ref, weight_ref).astype(jnp.bfloat16)
        spread_rows(spread_ref, cot_ref[block].reshape(512, cot_ref.shape[-1]))
        add_taps(total_ref, spread_ref, slab_ref)
        return carry

    lax.fori_loop(0, own_ref.shape[0], step, 0)
    write_taps(total_ref, grad_ref, scale)


def call(body, outs, scratch, flops, *operands):
    space = pl.BlockSpec(memory_space=pltpu.VMEM)
    specs = [pl.BlockSpec(memory_space=pltpu.SMEM)] + [space] * (len(operands) - 1)
    moved = sum(x.size * x.dtype.itemsize for x in operands)
    return pl.pallas_call(
        body,
        out_shape=outs,
        in_specs=specs,
        out_specs=[space] * len(outs),
        scratch_shapes=scratch,
        compiler_params=pltpu.CompilerParams(vmem_limit_bytes=VMEM_LIMIT),
        cost_estimate=pl.CostEstimate(flops=flops, bytes_accessed=moved, transcendentals=0),
    )(*operands)


def local(features, weight_one, weight_two, cotangent, neighbours):
    block_count, channels = features.shape[1], features.shape[3]
    devices = lax.axis_size("blocks")
    reach = (block_count + 24) // block_count
    own = features[0].reshape(block_count, 8, 64, channels)
    cot = cotangent[0].reshape(block_count, 8, 64, channels)
    links = neighbours[0]
    whole = devices <= 2 * reach + 1
    if whole:
        placed = links
    else:
        gap = links // block_count - lax.axis_index("blocks")
        placed = jnp.where(links >= 0, (gap + reach) * block_count + links % block_count, -1)

    def collect(payload):
        if whole:
            return lax.all_gather(payload, "blocks", axis=0, tiled=True)
        pieces = [
            payload if gap == 0 else from_behind(payload, "blocks", -gap)
            for gap in range(-reach, reach + 1)
        ]
        return jnp.concatenate(pieces, axis=0)

    def slabs(weights):
        return weights.reshape(3, 9 * channels, channels)

    flipped = jnp.transpose(weight_two[::-1], (0, 2, 1))
    voxels = lax.axis_size("rep") * devices * block_count * 512
    scale = 1.0 / math.sqrt(voxels)
    flops = 2 * block_count * 512 * 27 * channels * channels
    f32, bf16 = jnp.float32, jnp.bfloat16
    pad = pltpu.VMEM((3, 10, 80, channels), f32)
    slab = pltpu.VMEM((640, 9 * channels), bf16)
    spread = pltpu.VMEM((640, 3 * channels), bf16)
    total = pltpu.VMEM((3 * channels, 9 * channels), f32)
    rows = (block_count, 512, channels)
    grads = jax.ShapeDtypeStruct(weight_one.shape, f32)

    table = collect(own)
    cot_table = collect(cot)
    pre, hidden = call(
        first_kernel,
        [jax.ShapeDtypeStruct(rows, f32), jax.ShapeDtypeStruct(rows, bf16)],
        [pad, slab], flops,
        placed, own, table, slabs(weight_one),
    )
    hidden = hidden.reshape(own.shape)
    hidden_table = collect(hidden)
    (grad_one,) = call(
        functools.partial(back_kernel, scale),
        [grads], [pad, slab, spread, total], 2 * flops,
        placed, own, table, cot, cot_table, slabs(flipped), pre,
    )
    grad_one = lax.psum(grad_one, ("blocks", "rep"))
    out, grad_two = call(
        functools.partial(second_kernel, scale),
        [jax.ShapeDtypeStruct(rows, bf16), grads], [pad, slab, spread, total], 2 * flops,
        placed, hidden, hidden_table, cot, slabs(weight_two),
    )
    grad_two = lax.psum(grad_two, ("blocks", "rep"))
    return out.reshape(features.shape), grad_one, grad_two


def solution(mesh):
    in_specs = (
        P("rep", "blocks", None, None),
        P(),
        P(),
        P("rep", "blocks", None, None),
        P("rep", "blocks", None),
    )
    out_specs = (P("rep", "blocks", None, None), P(), P())
    return jax.shard_map(local, mesh=mesh, in_specs=in_specs, out_specs=out_specs, check_vma=False)
```

profile of v0, /device:TPU:1, one launch (start us, length us, event | category | flops | bytes accessed | tf_op | source)
XLA Modules:
  0.0 393.1 jit_solution(4176774016720889449)
XLA Ops:
  7.2 0.0 all-gather.4.cloned.1.call-start
  7.2 0.7 all-gather.4.cloned.1.call-update
  7.9 0.0 all-gather.8.cloned.1.call-start
  7.9 0.7 all-gather.8.cloned.1.call-update
  8.6 0.0 all-gather.6.cloned.1.call-start
  8.7 75.8 %all-gather.4.cloned.1.call-done.table_ref = bf16[32,8,64,128]{3,2,1,0:T(8,128)(2,1)} async-done(((bf16[4,8,64,128]{3,2,1,0:T(8,128)(2,1)}), bf16[32,8,64,128]{3,2,1,0:T(8,128)(2,1)}) %all-gather.4.cloned.1.call-update) | async-done | bytes 4194320 | tf_op jit(solution)/shard_map/all_gather | solution.py:194
  84.4 0.0 copy-start.1
  84.5 8.6 %shard_map.76 = (f32[4,512,128]{2,1,0:T(8,128)}, bf16[4,512,128]{2,1,0:T(8,128)(2,1)}) custom-call(s32[4,26]{1,0:T(4,128)} %bitcast.21, bf16[4,8,64,128]{3,2,1,0:T(8,128)(2,1)} %bitcast.13, bf16[32,8,64,128]{3,2,1,0:T(8,128)(2,1)} %all-gather.4.cloned.1.call-done.table_ref, bf16[3,1152,128]{2,1,0:T(8,128)(2,1)} %bitcast.20), custom_call_target="tpu_custom_call" | custom-call | flops 1811939328 | bytes 5603744 | tf_op jit(solution)/shard_map/pallas_call | solution.py:167
  93.1 0.0 all-gather.6.cloned.1.call-update
  93.1 0.0 all-reduce.3.cloned.1.call-start
  93.1 0.0 copy-done.1
  93.2 0.1 reverse_bitcast_fusion
  93.2 1.7 copy.9
  94.9 63.4 %all-gather.8.cloned.1.call-done.cot_table_ref = bf16[32,8,64,128]{3,2,1,0:T(8,128)(2,1)} async-done(((bf16[4,8,64,128]{3,2,1,0:T(8,128)(2,1)}), bf16[32,8,64,128]{3,2,1,0:T(8,128)(2,1)}) %all-gather.8.cloned.1.call-update) | async-done | bytes 4194320 | tf_op jit(solution)/shard_map/all_gather | solution.py:194
  158.3 16.8 %shard_map.78 = f32[27,128,128]{2,1,0:T(8,128)} custom-call(s32[4,26]{1,0:T(4,128)} %bitcast.22, bf16[4,8,64,128]{3,2,1,0:T(8,128)(2,1)} %bitcast.14, bf16[32,8,64,128]{3,2,1,0:T(8,128)(2,1)} %all-gather.4.cloned.1.call-done.table_ref, bf16[4,8,64,128]{3,2,1,0:T(8,128)(2,1)} %bitcast.16, bf16[32,8,64,128]{3,2,1,0:T(8,128)(2,1)} %all-gather.8.cloned.1.call-done.cot_table_ref, ...), custom_call_target="tpu_custom_call" | custom-call | flops 3623878656 | bytes 11370912 | tf_op jit(solution)/shard_map/pallas_call | solution.py:167
  175.1 57.0 %all-gather.6.cloned.1.call-done.table_ref = bf16[32,8,64,128]{3,2,1,0:T(8,128)(2,1)} async-done(((bf16[4,8,64,128]{3,2,1,0:T(8,128)(2,1)}), bf16[32,8,64,128]{3,2,1,0:T(8,128)(2,1)}) %all-gather.6.cloned.1.call-update) | async-done | bytes 4194320 | tf_op jit(solution)/shard_map/all_gather | solution.py:194
  232.1 12.6 %shard_map.77 = (bf16[4,512,128]{2,1,0:T(8,128)(2,1)}, f32[27,128,128]{2,1,0:T(8,128)}) custom-call(s32[4,26]{1,0:T(4,128)} %bitcast.23, bf16[4,8,64,128]{3,2,1,0:T(8,128)(2,1)} %bitcast.19, bf16[32,8,64,128]{3,2,1,0:T(8,128)(2,1)} %all-gather.6.cloned.1.call-done.table_ref, bf16[4,8,64,128]{3,2,1,0:T(8,128)(2,1)} %bitcast.17, bf16[3,1152,128]{2,1,0:T(8,128)(2,1)} %bitcast.10), custom_call_target="tpu_custom_call" | custom-call | flops 3623878656 | bytes 6128032 | tf_op jit(solution)/shard_map/pallas_call | solution.py:167
  244.7 0.0 all-reduce.3.cloned.1.call-update
  244.7 137.6 %all-reduce.3.cloned.1.call-done = (f32[27,128,128]{2,1,0:T(8,128)}, f32[27,128,128]{2,1,0:T(8,128)}) async-done(((f32[27,128,128]{2,1,0:T(8,128)}, f32[27,128,128]{2,1,0:T(8,128)}), (f32[27,128,128]{2,1,0:T(8,128)}, f32[27,128,128]{2,1,0:T(8,128)})) %all-reduce.3.cloned.1.call-update) | async-done | bytes 3538960 | tf_op jit(solution)/shard_map/psum | solution.py:231
  382.3 0.0 copy-start
  382.3 3.0 copy.12
  385.3 0.0 copy-done
  385.3 1.2 copy.13
Async XLA Ops:
  7.2 77.3 %all-gather.4.cloned.1.call-start = ((), (), s32[]{:S(2)}) async-start(), calls=%async_computation | async-start | bytes 4718592 | tf_op jit(solution)/shard_map/all_gather | solution.py:194
  7.9 150.4 %all-gather.8.cloned.1.call-start = ((), (), s32[]{:S(2)}) async-start(), calls=%async_computation.2 | async-start | bytes 4718592 | tf_op jit(solution)/shard_map/all_gather | solution.py:194
  8.6 223.4 %all-gather.6.cloned.1.call-start = ((), (), s32[]{:S(2)}) async-start(), calls=%async_computation.1 | async-start | bytes 4718592 | tf_op jit(solution)/shard_map/all_gather | solution.py:194
  84.4 8.7 %copy-start.1 = (bf16[27,128,128]{2,1,0:T(8,128)(2,1)S(1)}, bf16[27,128,128]{2,1,0:T(8,128)(2,1)}, u32[]{:S(2)}) copy-start(bf16[27,128,128]{2,1,0:T(8,128)(2,1)} %param.7) | copy-start | bytes 2654212
  93.1 289.2 %all-reduce.3.cloned.1.call-start = ((), (), s32[]{:S(2)}) async-start(), calls=%async_computation.3 | async-start | bytes 7077888 | tf_op jit(solution)/shard_map/psum | solution.py:231
  382.3 3.0 copy-start
Sparse Core Ops, SparseCore 0:
  10.1 74.2 all-gather.3
  86.6 71.6 all-gather.7
  160.4 71.6 all-gather.5
  244.8 137.4 all-reduce.2
where the time goes:
time: 395 us; the launch traced here: 393 us
  waiting for transfers between devices  335 us (85%)
  Pallas kernels  38 us (10%)
  between operations  13.8 us (3%)
  local copies, waits for them, and re-layouts  5.96 us (2%)
    all_gather x3, waiting for transfers between devices, collect(): return lax.all_gather(payload, 'blocks', axis=0, tiled=True)  196 us
    psum x1, waiting for transfers between devices, local(): grad_one = lax.psum(grad_one, ('blocks', 'rep'))  138 us
    pallas_call x3, Pallas kernels, call(): pl.pallas_call(body, out_shape=outs, in_specs=specs, out_specs=[space] *...  38 us
  transfers between devices with their start and end apart: 4, of which 4 were waited for; matrix products, arithmetic and copies ran while one was open for 0% of the time, Pallas kernels for 6%

commit v1 on v0

--- a/solution.py
+++ b/solution.py
@@ -26,23 +26,61 @@
     return rows.astype(jnp.float32).reshape(-1, 8, rows.shape[-1])
 
 
+def plane_start(plane):
+    return {0: 0, 7: 64}.get(plane, 128 + 32 * (plane - 1))
+
+
+def pack_shell(block, own_ref, shell_ref):
+    channels = own_ref.shape[-1]
+    for plane in (0, 7):
+        shell_ref[block, pl.ds(plane_start(plane), 64), :] = own_ref[block, plane]
+    for plane in range(1, 7):
+        lines = lines_of(own_ref[block, plane])
+        cell = lax.broadcasted_iota(jnp.int32, (1, 8, channels), 1)
+        ends = []
+        for group in (0, 4):
+            packed = pltpu.roll(lines[group : group + 1], 1, 1)
+            for turn in range(1, 4):
+                line = pltpu.roll(lines[group + turn : group + turn + 1], 2 * turn + 1, 1)
+                packed = jnp.where(cell >= 2 * turn, line, packed)
+            ends.append(packed)
+        packed = jnp.concatenate([lines[0:1], lines[7:8]] + ends, axis=0)
+        shell_ref[block, pl.ds(plane_start(plane), 32), :] = packed.reshape(32, channels).astype(
+            jnp.bfloat16
+        )
+
+
 def build_slab(block, own_ref, table_ref, place_ref, pad_ref, slab_ref):
     channels = own_ref.shape[-1]
 
-    def place(step_x, step_y, step_z):
-        return place_ref[block, offset_index(step_x, step_y, step_z)]
-
-    def source(step_x, step_y, step_z, plane, rows):
+    def source(step_x, step_y, step_z, plane):
         if (step_x, step_y, step_z) == (0, 0, 0):
-            return lines_of(own_ref[block, plane, rows, :])
-        where = place(step_x, step_y, step_z)
-        got = lines_of(table_ref[jnp.maximum(where, 0), plane, rows, :])
+            return lines_of(own_ref[block, plane])
+        where = place_ref[block, offset_index(step_x, step_y, step_z)]
+        near, start = jnp.maximum(where, 0), plane_start(plane)
+        if plane in (0, 7):
+            if step_y == 0:
+                got = lines_of(table_ref[near, pl.ds(start, 64), :])
+            elif step_y == 1:
+                got = lines_of(table_ref[near, pl.ds(start, 16), :])[0:1]
+            else:
+                got = lines_of(table_ref[near, pl.ds(start + 48, 16), :])[1:2]
+        elif step_y == 0:
+            ends = lines_of(table_ref[near, pl.ds(start + 16, 16), :])
+            got = jnp.concatenate(
+                [
+                    pltpu.roll(ends[j // 4 : j // 4 + 1], 7 - 2 * (j % 4), 1)
+                    for j in range(8)
+                ],
+                axis=0,
+            )
+        else:
+            got = lines_of(table_ref[near, pl.ds(start, 16), :])
+            got = got[0:1] if step_y == 1 else got[1:2]
         return jnp.where(where >= 0, got, 0.0)
 
-    def put(ii, first_line, step_x, step_y, plane, rows, pick):
-        mid, low, high = (
-            source(step_x, step_y, step_z, plane, rows)[pick] for step_z in (0, -1, 1)
-        )
+    def put(ii, first_line, step_x, step_y, plane):
+        mid, low, high = (source(step_x, step_y, step_z, plane) for step_z in (0, -1, 1))
         cell = lax.broadcasted_iota(jnp.int32, mid.shape, 1)
         count = mid.shape[0]
         shifted = (
@@ -55,13 +93,12 @@
                 8 * count, channels
             )
 
-    every = slice(None)
     for ii in range(10):
         step_x = -1 if ii == 0 else (1 if ii == 9 else 0)
         plane = 7 if ii == 0 else (0 if ii == 9 else ii - 1)
-        put(ii, 0, step_x, -1, plane, slice(48, 64), slice(1, 2))
-        put(ii, 1, step_x, 0, plane, slice(0, 64), every)
-        put(ii, 9, step_x, 1, plane, slice(0, 16), slice(0, 1))
+        put(ii, 0, step_x, -1, plane)
+        put(ii, 1, step_x, 0, plane)
+        put(ii, 9, step_x, 1, plane)
     for tap_b in range(3):
         for tap_c in range(3):
             column = (3 * tap_b + tap_c) * channels
@@ -111,12 +148,25 @@
     return 1.0 / (1.0 + jnp.exp(-values))
 
 
-def first_kernel(place_ref, own_ref, table_ref, weight_ref, pre_ref, hidden_ref, pad_ref, slab_ref):
+def pack_kernel(own_ref, cot_ref, own_shell_ref, cot_shell_ref):
+    def step(block, carry):
+        pack_shell(block, own_ref, own_shell_ref)
+        pack_shell(block, cot_ref, cot_shell_ref)
+        return carry
+
+    lax.fori_loop(0, own_ref.shape[0], step, 0)
+
+
+def first_kernel(
+    place_ref, own_ref, table_ref, weight_ref, pre_ref, hidden_ref, shell_ref, pad_ref, slab_ref
+):
     def step(block, carry):
         build_slab(block, own_ref, table_ref, place_ref, pad_ref, slab_ref)
         pre = conv_slab(slab_ref, weight_ref)
         pre_ref[block] = pre
-        hidden_ref[block] = (pre / (1.0 + jnp.exp(-pre))).astype(jnp.bfloat16)
+        hidden = (pre / (1.0 + jnp.exp(-pre))).astype(jnp.bfloat16)
+        hidden_ref[block] = hidden.reshape(hidden_ref.shape[1:])
+        pack_shell(block, hidden_ref, shell_ref)
         return carry
 
     lax.fori_loop(0, own_ref.shape[0], step, 0)
@@ -160,9 +210,186 @@
     write_taps(total_ref, grad_ref, scale)
 
 
+def ring_kernel(devices, payload_ref, table_ref, send_sem, recv_sem, own_sem):
+    count = payload_ref.shape[0]
+    half = count // 2
+    me = lax.axis_index("blocks")
+    odd = me % 2
+    pos = (1 - odd) * (me // 2) + odd * (devices - 1 - me // 2)
+
+    def index_of(position):
+        spot = (position + 2 * devices) % devices
+        back = spot // (devices // 2)
+        return (1 - back) * 2 * spot + back * (2 * (devices - 1 - spot) + 1)
+
+    ends = (index_of(pos + 1), index_of(pos - 1))
+    barrier = pltpu.get_barrier_semaphore()
+    for end in ends:
+        pl.semaphore_signal(
+            barrier, inc=1, device_id={"blocks": end}, device_id_type=pl.DeviceIdType.MESH
+        )
+    pl.semaphore_wait(barrier, 2)
+    own = pltpu.make_async_copy(payload_ref, table_ref.at[pl.ds(me * count, count)], own_sem)
+    own.start()
+    copies = []
+    for step in range(devices - 1):
+        for way, sign in ((0, 1), (1, -1)):
+            if step:
+                copies[2 * (step - 1) + way].wait_recv()
+            owner = index_of(pos - sign * step)
+            target = table_ref.at[pl.ds(owner * count + way * half, half)]
+            source = payload_ref.at[pl.ds(way * half, half)] if step == 0 else target
+            copy = pltpu.make_async_remote_copy(
+                src_ref=source,
+                dst_ref=target,
+                send_sem=send_sem.at[way, step],
+                recv_sem=recv_sem.at[way, step],
+                device_id={"blocks": ends[way]},
+                device_id_type=pl.DeviceIdType.MESH,
+            )
+            copy.start()
+            copies.append(copy)
+    for copy in copies[-2:]:
+        copy.wait_recv()
+    for copy in copies:
+        copy.wait_send()
+    own.wait()
+
+
+def ring_gather(payload, devices, collective_id):
+    space = pl.BlockSpec(memory_space=pltpu.VMEM)
+    sems = pltpu.SemaphoreType.DMA((2, devices - 1))
+    return pl.pallas_call(
+        functools.partial(ring_kernel, devices),
+        out_shape=jax.ShapeDtypeStruct(
+            (devices * payload.shape[0],) + payload.shape[1:], payload.dtype
+        ),
+        in_specs=[space],
+        out_specs=space,
+        scratch_shapes=[sems, sems, pltpu.SemaphoreType.DMA],
+        compiler_params=pltpu.CompilerParams(
+            collective_id=collective_id, has_side_effects=True, vmem_limit_bytes=VMEM_LIMIT
+        ),
+    )(payload)
+
+
+def bit_orders(block_bits, rep_bits):
+    first = [("rep", 0)]
+    rest = [("rep", k) for k in range(1, rep_bits)]
+    low = [("blocks", k) for k in range(block_bits - 1)]
+    last = [("blocks", block_bits - 1)]
+    turning = rest + low
+    turns = [turning[t % len(turning) :] + turning[: t % len(turning)] for t in range(3)]
+    return [first + turn + last for turn in turns]
+
+
+def sum_kernel(orders, one_ref, two_ref, out_ref, held_ref, land_ref, send_sem, recv_sem):
+    rows = out_ref.shape[0]
+    share = rows // len(orders)
+    levels = len(orders[0])
+    place = {axis: lax.axis_index(axis) for axis in ("blocks", "rep")}
+
+    def bit_of(dim):
+        axis, k = dim
+        return place[axis] // 2**k % 2
+
+    def partner(dim):
+        axis, k = dim
+        return {axis: place[axis] + (1 - 2 * bit_of(dim)) * 2**k}
+
+    barrier = pltpu.get_barrier_semaphore()
+    for dim in orders[0]:
+        pl.semaphore_signal(
+            barrier, inc=1, device_id=partner(dim), device_id_type=pl.DeviceIdType.MESH
+        )
+    pl.semaphore_wait(barrier, levels)
+    held_ref[pl.ds(0, rows // 2), :] = one_ref[...]
+    held_ref[pl.ds(rows // 2, rows // 2), :] = two_ref[...]
+
+    def copy_to(part, step, dim, source, target):
+        return pltpu.make_async_remote_copy(
+            src_ref=source,
+            dst_ref=target,
+            send_sem=send_sem.at[part, step],
+            recv_sem=recv_sem.at[part, step],
+            device_id=partner(dim),
+            device_id_type=pl.DeviceIdType.MESH,
+        )
+
+    starts = [[part * share] for part in range(len(orders))]
+    flying = [None] * len(orders)
+    sent = []
+    for step in range(levels + 1):
+        half = share >> (step + 1)
+        for part, order in enumerate(orders):
+            if step:
+                flying[part].wait_recv()
+                size = share >> step
+                mine = pl.ds(pl.multiple_of(starts[part][-1], 8), size)
+                landed = pl.ds(part * share + share - 2 * size, size)
+                summed = held_ref[mine, :] + land_ref[landed, :]
+                kept_ref = held_ref if step < levels else out_ref
+                kept_ref[mine, :] = summed
+            if step < levels:
+                bit = bit_of(order[step])
+                start = starts[part][-1]
+                away = pl.multiple_of(start + (1 - bit) * half, 8)
+                copy = copy_to(
+                    part, step, order[step],
+                    held_ref.at[pl.ds(away, half)],
+                    land_ref.at[pl.ds(part * share + share - 2 * half, half)],
+                )
+                copy.start()
+                flying[part] = copy
+                sent.append(copy)
+                starts[part].append(start + bit * half)
+    for step in reversed(range(levels)):
+        size = share >> (step + 1)
+        for part, order in enumerate(orders):
+            if step < levels - 1:
+                flying[part].wait_recv()
+            mine = out_ref.at[pl.ds(pl.multiple_of(starts[part][step + 1], 8), size)]
+            copy = copy_to(part, levels + step, order[step], mine, mine)
+            copy.start()
+            flying[part] = copy
+            sent.append(copy)
+    for copy in flying:
+        copy.wait_recv()
+    for copy in sent:
+        copy.wait_send()
+
+
+def sum_everywhere(one, two, block_devices, rep_devices, collective_id):
+    block_bits, rep_bits = block_devices.bit_length() - 1, rep_devices.bit_length() - 1
+    orders = bit_orders(block_bits, rep_bits)
+    channels = one.shape[-1]
+    rows = 2 * one.size // channels
+    space = pl.BlockSpec(memory_space=pltpu.VMEM)
+    sems = pltpu.SemaphoreType.DMA((len(orders), 2 * len(orders[0])))
+    out = pl.pallas_call(
+        functools.partial(sum_kernel, orders),
+        out_shape=jax.ShapeDtypeStruct((rows, channels), one.dtype),
+        in_specs=[space, space],
+        out_specs=space,
+        scratch_shapes=[pltpu.VMEM((rows, channels), one.dtype)] * 2 + [sems, sems],
+        compiler_params=pltpu.CompilerParams(
+            collective_id=collective_id, has_side_effects=True, vmem_limit_bytes=VMEM_LIMIT
+        ),
+    )(one.reshape(-1, channels), two.reshape(-1, channels))
+    return out[: rows // 2].reshape(one.shape), out[rows // 2 :].reshape(two.shape)
+
+
+def can_halve(count, rows):
+    block_devices, rep_devices = count
+    total = block_devices * rep_devices
+    powers = total & (total - 1) == 0 and block_devices >= 2 and rep_devices >= 2
+    return powers and rows % (3 * 8 * total) == 0
+
+
 def call(body, outs, scratch, flops, *operands):
     space = pl.BlockSpec(memory_space=pltpu.VMEM)
-    specs = [pl.BlockSpec(memory_space=pltpu.SMEM)] + [space] * (len(operands) - 1)
+    scalars = pl.BlockSpec(memory_space=pltpu.SMEM)
+    specs = [scalars if x.dtype == jnp.int32 else space for x in operands]
     moved = sum(x.size * x.dtype.itemsize for x in operands)
     return pl.pallas_call(
         body,
@@ -189,7 +416,11 @@
         gap = links // block_count - lax.axis_index("blocks")
         placed = jnp.where(links >= 0, (gap + reach) * block_count + links % block_count, -1)
 
-    def collect(payload):
+    ring = whole and devices % 2 == 0 and block_count % 2 == 0
+
+    def collect(payload, collective_id=None):
+        if ring and collective_id is not None:
+            return ring_gather(payload, devices, collective_id)
         if whole:
             return lax.all_gather(payload, "blocks", axis=0, tiled=True)
         pieces = [
@@ -213,28 +444,34 @@
     rows = (block_count, 512, channels)
     grads = jax.ShapeDtypeStruct(weight_one.shape, f32)
 
-    table = collect(own)
-    cot_table = collect(cot)
-    pre, hidden = call(
+    shell = jax.ShapeDtypeStruct((block_count, 320, channels), bf16)
+
+    own_shell, cot_shell = call(pack_kernel, [shell, shell], [], 0, own, cot)
+    cot_table = collect(cot_shell)
+    table = collect(own_shell, 1)
+    pre, hidden, hidden_shell = call(
         first_kernel,
-        [jax.ShapeDtypeStruct(rows, f32), jax.ShapeDtypeStruct(rows, bf16)],
+        [jax.ShapeDtypeStruct(rows, f32), jax.ShapeDtypeStruct(own.shape, bf16), shell],
         [pad, slab], flops,
         placed, own, table, slabs(weight_one),
     )
-    hidden = hidden.reshape(own.shape)
-    hidden_table = collect(hidden)
+    hidden_table = collect(hidden_shell, 2)
+    out, grad_two = call(
+        functools.partial(second_kernel, scale),
+        [jax.ShapeDtypeStruct(rows, bf16), grads], [pad, slab, spread, total], 2 * flops,
+        placed, hidden, hidden_table, cot, slabs(weight_two),
+    )
+    cot_table, grad_two = lax.optimization_barrier((cot_table, grad_two))
     (grad_one,) = call(
         functools.partial(back_kernel, scale),
         [grads], [pad, slab, spread, total], 2 * flops,
         placed, own, table, cot, cot_table, slabs(flipped), pre,
     )
-    grad_one = lax.psum(grad_one, ("blocks", "rep"))
-    out, grad_two = call(
-        functools.partial(second_kernel, scale),
-        [jax.ShapeDtypeStruct(rows, bf16), grads], [pad, slab, spread, total], 2 * flops,
-        placed, hidden, hidden_table, cot, slabs(weight_two),
-    )
-    grad_two = lax.psum(grad_two, ("blocks", "rep"))
+    counts = (devices, lax.axis_size("rep"))
+    if can_halve(counts, 2 * grad_one.size // channels):
+        grad_one, grad_two = sum_everywhere(grad_one, grad_two, *counts, 3)
+    else:
+        grad_one, grad_two = lax.psum((grad_one, grad_two), ("blocks", "rep"))
     return out.reshape(features.shape), grad_one, grad_two
 
 

time: 395 us -> 216 us (0.55)
  waiting for transfers between devices: 335 us -> 0.02 us
  Pallas kernels: 38 us -> 196 us
    all_gather x3 -> x1, waiting for transfers between devices: 196 us -> 0.01 us  [collect(): return lax.all_gather(payload, 'blocks', axis=0, tiled=True)]
    pallas_call x0 -> x3, Pallas kernels: none -> 157 us  [the longest x2 85.8 us: ring_gather(): pl.pallas_call(functools.partial(ring_kernel, devices), out_shape=jax.Sha...]
    psum x1 -> x0, waiting for transfers between devices: 138 us -> none  [local(): grad_one = lax.psum(grad_one, ('blocks', 'rep'))]
    unnamed x6 -> x2, local copies, waits for them, and re-layouts: 4.22 us -> 0.01 us
    slice x0 -> x1, local copies, waits for them, and re-layouts: none -> 4.03 us  [sum_everywhere(): out[rows // 2:].reshape(two.shape)]
    pallas_call x3 -> x4, Pallas kernels: 38 us -> 38.6 us  [call(): pl.pallas_call(body, out_shape=outs, in_specs=specs, out_specs=[space] *...]
  transfers between devices with their start and end apart: 4 -> 1, of which waited for: 4 -> 0; matrix products, arithmetic and copies ran while one was open for 0% -> 1% of each run, Pallas kernels for 6% -> 49%
where the time goes in v1:
time: 216 us
  Pallas kernels  196 us (91%)
  between operations  14.1 us (7%)
  local copies, waits for them, and re-layouts  5.75 us (3%)
    pallas_call x2, Pallas kernels, ring_gather(): pl.pallas_call(functools.partial(ring_kernel, devices), out_shape=jax.Sha...  85.8 us
    pallas_call x1, Pallas kernels, sum_everywhere(): pl.pallas_call(functools.partial(sum_kernel, orders), out_shape=jax.Shape...  71.5 us
    pallas_call x4, Pallas kernels, call(): pl.pallas_call(body, out_shape=outs, in_specs=specs, out_specs=[space] *...  38.6 us
  transfers between devices with their start and end apart: 1, of which 0 were waited for; matrix products, arithmetic and copies ran while one was open for 1% of the time, Pallas kernels for 49%

profile of v1, /device:TPU:1, one launch (start us, length us, event | category | flops | bytes accessed | tf_op | source)
XLA Modules:
  0.0 215.7 jit_solution(3275578814052840700)
XLA Ops:
  7.2 0.0 all-gather.2.cloned.1.call-start
  7.2 2.2 %shard_map.76 = (bf16[4,320,128]{2,1,0:T(8,128)(2,1)}, bf16[4,320,128]{2,1,0:T(8,128)(2,1)}) custom-call(bf16[4,8,64,128]{3,2,1,0:T(8,128)(2,1)} %bitcast.19, bf16[4,8,64,128]{3,2,1,0:T(8,128)(2,1)} %bitcast.22), custom_call_target="tpu_custom_call" | custom-call | bytes 1048576 | tf_op jit(solution)/shard_map/pallas_call | solution.py:394
  9.4 0.0 all-gather.2.cloned.1.call-update
  9.5 50.5 %shard_map.77.table_ref = bf16[32,320,128]{2,1,0:T(8,128)(2,1)} custom-call(bf16[4,320,128]{2,1,0:T(8,128)(2,1)} %get-tuple-element.12.payload_ref), custom_call_target="tpu_custom_call" | custom-call | tf_op jit(solution)/shard_map/pallas_call | solution.py:262
  60.0 8.4 %shard_map.78 = (f32[4,512,128]{2,1,0:T(8,128)}, bf16[4,8,64,128]{3,2,1,0:T(8,128)(2,1)}, bf16[4,320,128]{2,1,0:T(8,128)(2,1)}) custom-call(s32[4,26]{1,0:T(4,128)} %bitcast.26, bf16[4,8,64,128]{3,2,1,0:T(8,128)(2,1)} %bitcast.20, bf16[32,320,128]{2,1,0:T(8,128)(2,1)} %shard_map.77.table_ref, bf16[3,1152,128]{2,1,0:T(8,128)(2,1)} %bitcast.25), custom_call_target="tpu_custom_call" | custom-call | flops 1811939328 | bytes 4030880 | tf_op jit(solution)/shard_map/pallas_call | solution.py:394
  68.4 0.0 copy-start
  68.4 35.3 %shard_map.79.table_ref = bf16[32,320,128]{2,1,0:T(8,128)(2,1)} custom-call(bf16[4,320,128]{2,1,0:T(8,128)(2,1)} %get-tuple-element.14.payload_ref), custom_call_target="tpu_custom_call" | custom-call | tf_op jit(solution)/shard_map/pallas_call | solution.py:262
  103.6 0.0 copy-done
  103.6 0.1 reverse_bitcast_fusion
  103.7 1.6 copy.9
  105.4 12.1 %shard_map.80 = (bf16[4,512,128]{2,1,0:T(8,128)(2,1)}, f32[27,128,128]{2,1,0:T(8,128)}) custom-call(s32[4,26]{1,0:T(4,128)} %bitcast.27, bf16[4,8,64,128]{3,2,1,0:T(8,128)(2,1)} %get-tuple-element.13.own_ref, bf16[32,320,128]{2,1,0:T(8,128)(2,1)} %shard_map.79.table_ref, bf16[4,8,64,128]{3,2,1,0:T(8,128)(2,1)} %bitcast.23, bf16[3,1152,128]{2,1,0:T(8,128)(2,1)} %bitcast.17), custom_call_target="tpu_custom_call" | custom-call | flops 3623878656 | bytes 4555168 | tf_op jit(solution)/shard_map/pallas_call | solution.py:394
  117.5 0.0 all-gather.2.cloned.1.call-done.cot_table_ref
  117.5 15.9 %shard_map.81 = f32[27,128,128]{2,1,0:T(8,128)} custom-call(s32[4,26]{1,0:T(4,128)} %bitcast.28, bf16[4,8,64,128]{3,2,1,0:T(8,128)(2,1)} %bitcast.21, bf16[32,320,128]{2,1,0:T(8,128)(2,1)} %shard_map.77.table_ref, bf16[4,8,64,128]{3,2,1,0:T(8,128)(2,1)} %bitcast.24, bf16[32,320,128]{2,1,0:T(8,128)(2,1)} %all-gather.2.cloned.1.call-done.cot_table_ref, ...), custom_call_target="tpu_custom_call" | custom-call | flops 3623878656 | bytes 8225184 | tf_op jit(solution)/shard_map/pallas_call | solution.py:394
  133.4 71.5 %shard_map.82 = f32[6912,128]{1,0:T(8,128)} custom-call(f32[3456,128]{1,0:T(8,128)} %bitcast.16, f32[3456,128]{1,0:T(8,128)} %bitcast.13), custom_call_target="tpu_custom_call" | custom-call | tf_op jit(solution)/shard_map/pallas_call | solution.py:369
  204.8 4.0 %fusion = (f32[3456,128]{1,0:T(8,128)}, f32[3456,128]{1,0:T(8,128)}) fusion(f32[6912,128]{1,0:T(8,128)} %shard_map.82), kind=kLoop, calls=%fused_computation.1 | loop fusion | bytes 7077888 | tf_op jit(solution)/shard_map/slice | solution.py:379
Async XLA Ops:
  7.2 110.3 %all-gather.2.cloned.1.call-start = ((), (), s32[]{:S(2)}) async-start(), calls=%async_computation | async-start | bytes 2949120 | tf_op jit(solution)/shard_map/all_gather | solution.py:425
  68.4 35.3 %copy-start = (bf16[27,128,128]{2,1,0:T(8,128)(2,1)S(1)}, bf16[27,128,128]{2,1,0:T(8,128)(2,1)}, u32[]{:S(2)}) copy-start(bf16[27,128,128]{2,1,0:T(8,128)(2,1)} %param.7) | copy-start | bytes 2654212
Sparse Core Ops, SparseCore 0:
  10.2 68.4 all-gather.1

commit v2 on v1

--- a/solution.py
+++ b/solution.py
@@ -9,6 +9,8 @@
 from jax.sharding import PartitionSpec as P
 
 VMEM_LIMIT = 56 * 1024 * 1024
+SHELL = 320
+CUTS = 2
 
 
 def offset_index(step_x, step_y, step_z):
@@ -30,10 +32,10 @@
     return {0: 0, 7: 64}.get(plane, 128 + 32 * (plane - 1))
 
 
-def pack_shell(block, own_ref, shell_ref):
+def pack_shell(block, own_ref, shell_ref, base=0):
     channels = own_ref.shape[-1]
     for plane in (0, 7):
-        shell_ref[block, pl.ds(plane_start(plane), 64), :] = own_ref[block, plane]
+        shell_ref[block, pl.ds(base + plane_start(plane), 64), :] = own_ref[block, plane]
     for plane in range(1, 7):
         lines = lines_of(own_ref[block, plane])
         cell = lax.broadcasted_iota(jnp.int32, (1, 8, channels), 1)
@@ -45,19 +47,18 @@
                 packed = jnp.where(cell >= 2 * turn, line, packed)
             ends.append(packed)
         packed = jnp.concatenate([lines[0:1], lines[7:8]] + ends, axis=0)
-        shell_ref[block, pl.ds(plane_start(plane), 32), :] = packed.reshape(32, channels).astype(
-            jnp.bfloat16
-        )
-
-
-def build_slab(block, own_ref, table_ref, place_ref, pad_ref, slab_ref):
+        packed = packed.reshape(32, channels).astype(jnp.bfloat16)
+        shell_ref[block, pl.ds(base + plane_start(plane), 32), :] = packed
+
+
+def build_slab(block, own_ref, table_ref, place_ref, pad_ref, slab_ref, base=0):
     channels = own_ref.shape[-1]
 
     def source(step_x, step_y, step_z, plane):
         if (step_x, step_y, step_z) == (0, 0, 0):
             return lines_of(own_ref[block, plane])
         where = place_ref[block, offset_index(step_x, step_y, step_z)]
-        near, start = jnp.maximum(where, 0), plane_start(plane)
+        near, start = jnp.maximum(where, 0), base + plane_start(plane)
         if plane in (0, 7):
             if step_y == 0:
                 got = lines_of(table_ref[near, pl.ds(start, 64), :])
@@ -148,10 +149,10 @@
     return 1.0 / (1.0 + jnp.exp(-values))
 
 
-def pack_kernel(own_ref, cot_ref, own_shell_ref, cot_shell_ref):
+def pack_kernel(own_ref, cot_ref, shell_ref):
     def step(block, carry):
-        pack_shell(block, own_ref, own_shell_ref)
-        pack_shell(block, cot_ref, cot_shell_ref)
+        pack_shell(block, own_ref, shell_ref)
+        pack_shell(block, cot_ref, shell_ref, SHELL)
         return carry
 
     lax.fori_loop(0, own_ref.shape[0], step, 0)
@@ -172,25 +173,56 @@
     lax.fori_loop(0, own_ref.shape[0], step, 0)
 
 
-def back_kernel(
-    scale, place_ref, own_ref, table_ref, cot_ref, cot_table_ref, weight_ref, pre_ref,
-    grad_ref, pad_ref, slab_ref, spread_ref, total_ref,
+def back_step(
+    block, place_ref, own_ref, table_ref, cot_ref, weight_ref, pre_ref,
+    pad_ref, slab_ref, spread_ref, total_ref,
 ):
+    build_slab(block, cot_ref, table_ref, place_ref, pad_ref, slab_ref, SHELL)
+    back = conv_slab(slab_ref, weight_ref)
+    pre = pre_ref[block]
+    sig = sigmoid(pre)
+    delta = (back * (sig * (1.0 + pre * (1.0 - sig)))).astype(jnp.bfloat16)
+    spread_rows(spread_ref, delta)
+    build_slab(block, own_ref, table_ref, place_ref, pad_ref, slab_ref)
+    add_taps(total_ref, spread_ref, slab_ref)
+
+
+def back_kernel(scale, place_ref, own_ref, table_ref, cot_ref, weight_ref, pre_ref, grad_ref, *scratch):
+    total_ref = scratch[-1]
     total_ref[...] = jnp.zeros_like(total_ref)
 
     def step(block, carry):
-        build_slab(block, cot_ref, cot_table_ref, place_ref, pad_ref, slab_ref)
-        back = conv_slab(slab_ref, weight_ref)
-        pre = pre_ref[block]
-        sig = sigmoid(pre)
-        delta = (back * (sig * (1.0 + pre * (1.0 - sig)))).astype(jnp.bfloat16)
-        spread_rows(spread_ref, delta)
-        build_slab(block, own_ref, table_ref, place_ref, pad_ref, slab_ref)
-        add_taps(total_ref, spread_ref, slab_ref)
+        back_step(
+            block, place_ref, own_ref, table_ref, cot_ref, weight_ref, pre_ref, *scratch
+        )
         return carry
 
     lax.fori_loop(0, own_ref.shape[0], step, 0)
     write_taps(total_ref, grad_ref, scale)
+
+
+def back_ring_kernel(
+    scale, devices, place_ref, own_ref, table_ref, cot_ref, weight_ref, pre_ref, payload_ref,
+    grad_ref, hidden_table_ref, pad_ref, slab_ref, spread_ref, total_ref, *sems,
+):
+    begin, advance, finish = ring(devices, payload_ref, hidden_table_ref, *sems)
+    begin()
+    total_ref[...] = jnp.zeros_like(total_ref)
+    count = own_ref.shape[0]
+
+    def step(block, carry):
+        back_step(
+            block, place_ref, own_ref, table_ref, cot_ref, weight_ref, pre_ref,
+            pad_ref, slab_ref, spread_ref, total_ref,
+        )
+        advance(block, False)
+        return carry
+
+    lax.fori_loop(0, count, step, 0)
+    write_taps(total_ref, grad_ref, scale)
+    for later in range(count, devices - 1):
+        advance(later, later == devices - 2)
+    finish()
 
 
 def second_kernel(
@@ -210,12 +242,14 @@
     write_taps(total_ref, grad_ref, scale)
 
 
-def ring_kernel(devices, payload_ref, table_ref, send_sem, recv_sem, own_sem):
+def ring(devices, payload_ref, table_ref, send_sem, recv_sem, own_sem):
     count = payload_ref.shape[0]
     half = count // 2
+    cut = payload_ref.shape[1] // CUTS
     me = lax.axis_index("blocks")
     odd = me % 2
     pos = (1 - odd) * (me // 2) + odd * (devices - 1 - me // 2)
+    pieces = [(part, way) for part in range(half * CUTS) for way in range(2)]
 
     def index_of(position):
         spot = (position + 2 * devices) % devices
@@ -223,54 +257,63 @@
         return (1 - back) * 2 * spot + back * (2 * (devices - 1 - spot) + 1)
 
     ends = (index_of(pos + 1), index_of(pos - 1))
-    barrier = pltpu.get_barrier_semaphore()
-    for end in ends:
-        pl.semaphore_signal(
-            barrier, inc=1, device_id={"blocks": end}, device_id_type=pl.DeviceIdType.MESH
-        )
-    pl.semaphore_wait(barrier, 2)
     own = pltpu.make_async_copy(payload_ref, table_ref.at[pl.ds(me * count, count)], own_sem)
-    own.start()
-    copies = []
+
+    def copy_at(step, part, way, first):
+        owner = index_of(pos - (1 - 2 * way) * step)
+        block = way * half + part // CUTS
+        rows = pl.ds(part % CUTS * cut, cut)
+        target = table_ref.at[owner * count + block, rows]
+        return pltpu.make_async_remote_copy(
+            src_ref=payload_ref.at[block, rows] if first else target,
+            dst_ref=target,
+            send_sem=send_sem.at[way, step, part],
+            recv_sem=recv_sem.at[way, step, part],
+            device_id={"blocks": ends[way]},
+            device_id_type=pl.DeviceIdType.MESH,
+        )
+
+    def begin():
+        barrier = pltpu.get_barrier_semaphore()
+        for end in ends:
+            pl.semaphore_signal(
+                barrier, inc=1, device_id={"blocks": end}, device_id_type=pl.DeviceIdType.MESH
+            )
+        pl.semaphore_wait(barrier, 2)
+        for part, way in pieces:
+            copy_at(0, part, way, True).start()
+        own.start()
+
+    def advance(step, last):
+        for part, way in pieces:
+            copy_at(step, part, way, False).wait_recv()
+            if not last:
+                copy_at(step + 1, part, way, False).start()
+
+    def finish():
+        for step in range(devices - 1):
+            for part, way in pieces:
+                copy_at(step, part, way, step == 0).wait_send()
+        own.wait()
+
+    return begin, advance, finish
+
+
+def ring_kernel(devices, payload_ref, table_ref, *sems):
+    begin, advance, finish = ring(devices, payload_ref, table_ref, *sems)
+    begin()
     for step in range(devices - 1):
-        for way, sign in ((0, 1), (1, -1)):
-            if step:
-                copies[2 * (step - 1) + way].wait_recv()
-            owner = index_of(pos - sign * step)
-            target = table_ref.at[pl.ds(owner * count + way * half, half)]
-            source = payload_ref.at[pl.ds(way * half, half)] if step == 0 else target
-            copy = pltpu.make_async_remote_copy(
-                src_ref=source,
-                dst_ref=target,
-                send_sem=send_sem.at[way, step],
-                recv_sem=recv_sem.at[way, step],
-                device_id={"blocks": ends[way]},
-                device_id_type=pl.DeviceIdType.MESH,
-            )
-            copy.start()
-            copies.append(copy)
-    for copy in copies[-2:]:
-        copy.wait_recv()
-    for copy in copies:
-        copy.wait_send()
-    own.wait()
-
-
-def ring_gather(payload, devices, collective_id):
-    space = pl.BlockSpec(memory_space=pltpu.VMEM)
-    sems = pltpu.SemaphoreType.DMA((2, devices - 1))
-    return pl.pallas_call(
-        functools.partial(ring_kernel, devices),
-        out_shape=jax.ShapeDtypeStruct(
-            (devices * payload.shape[0],) + payload.shape[1:], payload.dtype
-        ),
-        in_specs=[space],
-        out_specs=space,
-        scratch_shapes=[sems, sems, pltpu.SemaphoreType.DMA],
-        compiler_params=pltpu.CompilerParams(
-            collective_id=collective_id, has_side_effects=True, vmem_limit_bytes=VMEM_LIMIT
-        ),
-    )(payload)
+        advance(step, step == devices - 2)
+    finish()
+
+
+def ring_sems(devices, count):
+    sems = pltpu.SemaphoreType.DMA((2, devices - 1, count // 2 * CUTS))
+    return [sems, sems, pltpu.SemaphoreType.DMA]
+
+
+def ring_table(payload, devices):
+    return jax.ShapeDtypeStruct((devices * payload.shape[0],) + payload.shape[1:], payload.dtype)
 
 
 def bit_orders(block_bits, rep_bits):
@@ -280,13 +323,15 @@
     last = [("blocks", block_bits - 1)]
     turning = rest + low
     turns = [turning[t % len(turning) :] + turning[: t % len(turning)] for t in range(3)]
-    return [first + turn + last for turn in turns]
+    return [first + turn + last for turn in turns] * 2
 
 
 def sum_kernel(orders, one_ref, two_ref, out_ref, held_ref, land_ref, send_sem, recv_sem):
     rows = out_ref.shape[0]
-    share = rows // len(orders)
     levels = len(orders[0])
+    unit, parts = 8 << levels, len(orders)
+    cuts = [unit * (rows // unit * part // parts) for part in range(parts + 1)]
+    shares = [cuts[part + 1] - cuts[part] for part in range(parts)]
     place = {axis: lax.axis_index(axis) for axis in ("blocks", "rep")}
 
     def bit_of(dim):
@@ -316,17 +361,17 @@
             device_id_type=pl.DeviceIdType.MESH,
         )
 
-    starts = [[part * share] for part in range(len(orders))]
+    starts = [[cuts[part]] for part in range(parts)]
     flying = [None] * len(orders)
     sent = []
     for step in range(levels + 1):
-        half = share >> (step + 1)
         for part, order in enumerate(orders):
+            half = shares[part] >> (step + 1)
             if step:
                 flying[part].wait_recv()
-                size = share >> step
+                size = shares[part] >> step
                 mine = pl.ds(pl.multiple_of(starts[part][-1], 8), size)
-                landed = pl.ds(part * share + share - 2 * size, size)
+                landed = pl.ds(cuts[part + 1] - 2 * size, size)
                 summed = held_ref[mine, :] + land_ref[landed, :]
                 kept_ref = held_ref if step < levels else out_ref
                 kept_ref[mine, :] = summed
@@ -337,15 +382,15 @@
                 copy = copy_to(
                     part, step, order[step],
                     held_ref.at[pl.ds(away, half)],
-                    land_ref.at[pl.ds(part * share + share - 2 * half, half)],
+                    land_ref.at[pl.ds(cuts[part + 1] - 2 * half, half)],
                 )
                 copy.start()
                 flying[part] = copy
                 sent.append(copy)
                 starts[part].append(start + bit * half)
     for step in reversed(range(levels)):
-        size = share >> (step + 1)
         for part, order in enumerate(orders):
+            size = shares[part] >> (step + 1)
             if step < levels - 1:
                 flying[part].wait_recv()
             mine = out_ref.at[pl.ds(pl.multiple_of(starts[part][step + 1], 8), size)]
@@ -383,10 +428,10 @@
     block_devices, rep_devices = count
     total = block_devices * rep_devices
     powers = total & (total - 1) == 0 and block_devices >= 2 and rep_devices >= 2
-    return powers and rows % (3 * 8 * total) == 0
-
-
-def call(body, outs, scratch, flops, *operands):
+    return powers and rows % (8 * total) == 0 and rows >= 6 * 8 * total
+
+
+def call(body, outs, scratch, flops, *operands, **params):
     space = pl.BlockSpec(memory_space=pltpu.VMEM)
     scalars = pl.BlockSpec(memory_space=pltpu.SMEM)
     specs = [scalars if x.dtype == jnp.int32 else space for x in operands]
@@ -397,7 +442,7 @@
         in_specs=specs,
         out_specs=[space] * len(outs),
         scratch_shapes=scratch,
-        compiler_params=pltpu.CompilerParams(vmem_limit_bytes=VMEM_LIMIT),
+        compiler_params=pltpu.CompilerParams(vmem_limit_bytes=VMEM_LIMIT, **params),
         cost_estimate=pl.CostEstimate(flops=flops, bytes_accessed=moved, transcendentals=0),
     )(*operands)
 
@@ -416,11 +461,16 @@
         gap = links // block_count - lax.axis_index("blocks")
         placed = jnp.where(links >= 0, (gap + reach) * block_count + links % block_count, -1)
 
-    ring = whole and devices % 2 == 0 and block_count % 2 == 0
-
-    def collect(payload, collective_id=None):
-        if ring and collective_id is not None:
-            return ring_gather(payload, devices, collective_id)
+    ringed = whole and devices % 2 == 0 and block_count % 2 == 0
+
+    def collect(payload, collective_id):
+        if ringed:
+            (table,) = call(
+                functools.partial(ring_kernel, devices),
+                [ring_table(payload, devices)], ring_sems(devices, block_count), 0, payload,
+                collective_id=collective_id, has_side_effects=True,
+            )
+            return table
         if whole:
             return lax.all_gather(payload, "blocks", axis=0, tiled=True)
         pieces = [
@@ -444,28 +494,36 @@
     rows = (block_count, 512, channels)
     grads = jax.ShapeDtypeStruct(weight_one.shape, f32)
 
-    shell = jax.ShapeDtypeStruct((block_count, 320, channels), bf16)
-
-    own_shell, cot_shell = call(pack_kernel, [shell, shell], [], 0, own, cot)
-    cot_table = collect(cot_shell)
-    table = collect(own_shell, 1)
+    shell = jax.ShapeDtypeStruct((block_count, SHELL, channels), bf16)
+    both = jax.ShapeDtypeStruct((block_count, 2 * SHELL, channels), bf16)
+
+    (shells,) = call(pack_kernel, [both], [], 0, own, cot)
+    table = collect(shells, 1)
     pre, hidden, hidden_shell = call(
         first_kernel,
         [jax.ShapeDtypeStruct(rows, f32), jax.ShapeDtypeStruct(own.shape, bf16), shell],
         [pad, slab], flops,
         placed, own, table, slabs(weight_one),
     )
-    hidden_table = collect(hidden_shell, 2)
+    back_operands = (placed, own, table, cot, slabs(flipped), pre)
+    back_scratch = [pad, slab, spread, total]
+    if ringed and block_count < devices - 1:
+        grad_one, hidden_table = call(
+            functools.partial(back_ring_kernel, scale, devices),
+            [grads, ring_table(hidden_shell, devices)],
+            back_scratch + ring_sems(devices, block_count), 2 * flops,
+            *back_operands, hidden_shell,
+            collective_id=2, has_side_effects=True,
+        )
+    else:
+        hidden_table = collect(hidden_shell, 2)
+        (grad_one,) = call(
+            functools.partial(back_kernel, scale), [grads], back_scratch, 2 * flops, *back_operands
+        )
     out, grad_two = call(
         functools.partial(second_kernel, scale),
         [jax.ShapeDtypeStruct(rows, bf16), grads], [pad, slab, spread, total], 2 * flops,
         placed, hidden, hidden_table, cot, slabs(weight_two),
-    )
-    cot_table, grad_two = lax.optimization_barrier((cot_table, grad_two))
-    (grad_one,) = call(
-        functools.partial(back_kernel, scale),
-        [grads], [pad, slab, spread, total], 2 * flops,
-        placed, own, table, cot, cot_table, slabs(flipped), pre,
     )
     counts = (devices, lax.axis_size("rep"))
     if can_halve(counts, 2 * grad_one.size // channels):

time: 216 us -> 172 us (0.80)
  Pallas kernels: 196 us -> 165 us
  between operations: 14.1 us -> 0.67 us
    pallas_call x2 -> x0, Pallas kernels: 85.8 us -> none  [ring_gather(): pl.pallas_call(functools.partial(ring_kernel, devices), out_shape=jax.Sha...]
    pallas_call x4 -> x5, Pallas kernels: 38.6 us -> 114 us  [call(): pl.pallas_call(body, out_shape=outs, in_specs=specs, out_specs=[space] *...]
    pallas_call x1, Pallas kernels: 71.5 us -> 51.3 us  [sum_everywhere(): pl.pallas_call(functools.partial(sum_kernel, orders), out_shape=jax.Shape...]
  transfers between devices with their start and end apart: 1 -> 0, of which waited for: 0 -> 0; matrix products, arithmetic and copies ran while one was open for 1% -> 0% of each run, Pallas kernels for 49% -> 0%
where the time goes in v2:
time: 172 us
  Pallas kernels  165 us (96%)
  local copies, waits for them, and re-layouts  5.76 us (3%)
    pallas_call x5, Pallas kernels, call(): pl.pallas_call(body, out_shape=outs, in_specs=specs, out_specs=[space] *...  114 us
    pallas_call x1, Pallas kernels, sum_everywhere(): pl.pallas_call(functools.partial(sum_kernel, orders), out_shape=jax.Shape...  51.3 us
    slice x1, local copies, waits for them, and re-layouts, sum_everywhere(): out[rows // 2:].reshape(two.shape)  4.03 us

profile of v2, /device:TPU:1, one launch (start us, length us, event | category | flops | bytes accessed | tf_op | source)
XLA Modules:
  0.0 171.9 jit_solution(13281772347820503461)
XLA Ops:
  0.6 2.2 %shard_map.76.payload_ref = bf16[4,640,128]{2,1,0:T(8,128)(2,1)} custom-call(bf16[4,8,64,128]{3,2,1,0:T(8,128)(2,1)} %bitcast.19, bf16[4,8,64,128]{3,2,1,0:T(8,128)(2,1)} %bitcast.22), custom_call_target="tpu_custom_call" | custom-call | bytes 1048576 | tf_op jit(solution)/shard_map/pallas_call | solution.py:439
  2.9 57.2 %shard_map.77.table_ref = bf16[32,640,128]{2,1,0:T(8,128)(2,1)} custom-call(bf16[4,640,128]{2,1,0:T(8,128)(2,1)} %shard_map.76.payload_ref), custom_call_target="tpu_custom_call" | custom-call | bytes 655360 | tf_op jit(solution)/shard_map/pallas_call | solution.py:439
  60.0 0.0 copy-start
  60.0 9.2 %shard_map.78 = (f32[4,512,128]{2,1,0:T(8,128)}, bf16[4,8,64,128]{3,2,1,0:T(8,128)(2,1)}, bf16[4,320,128]{2,1,0:T(8,128)(2,1)}) custom-call(s32[4,26]{1,0:T(4,128)} %bitcast.26, bf16[4,8,64,128]{3,2,1,0:T(8,128)(2,1)} %bitcast.20, bf16[32,640,128]{2,1,0:T(8,128)(2,1)} %shard_map.77.table_ref, bf16[3,1152,128]{2,1,0:T(8,128)(2,1)} %bitcast.25), custom_call_target="tpu_custom_call" | custom-call | flops 1811939328 | bytes 6652320 | tf_op jit(solution)/shard_map/pallas_call | solution.py:439
  69.2 0.0 copy-done
  69.2 0.1 reverse_bitcast_fusion
  69.3 1.6 copy.8
  71.0 33.4 %shard_map.79 = (f32[27,128,128]{2,1,0:T(8,128)}, bf16[32,320,128]{2,1,0:T(8,128)(2,1)}) custom-call(s32[4,26]{1,0:T(4,128)} %bitcast.27, bf16[4,8,64,128]{3,2,1,0:T(8,128)(2,1)} %bitcast.21, bf16[32,640,128]{2,1,0:T(8,128)(2,1)} %shard_map.77.table_ref, bf16[4,8,64,128]{3,2,1,0:T(8,128)(2,1)} %bitcast.23, bf16[3,1152,128]{2,1,0:T(8,128)(2,1)} %bitcast.18, ...), custom_call_target="tpu_custom_call" | custom-call | flops 3623878656 | bytes 8552864 | tf_op jit(solution)/shard_map/pallas_call | solution.py:439
  104.4 12.1 %shard_map.80 = (bf16[4,512,128]{2,1,0:T(8,128)(2,1)}, f32[27,128,128]{2,1,0:T(8,128)}) custom-call(s32[4,26]{1,0:T(4,128)} %bitcast.28, bf16[4,8,64,128]{3,2,1,0:T(8,128)(2,1)} %get-tuple-element.10.own_ref, bf16[32,320,128]{2,1,0:T(8,128)(2,1)} %get-tuple-element.13.table_ref, bf16[4,8,64,128]{3,2,1,0:T(8,128)(2,1)} %bitcast.24, bf16[3,1152,128]{2,1,0:T(8,128)(2,1)} %bitcast.17), custom_call_target="tpu_custom_call" | custom-call | flops 3623878656 | bytes 4555168 | tf_op jit(solution)/shard_map/pallas_call | solution.py:439
  116.5 51.3 %shard_map.81 = f32[6912,128]{1,0:T(8,128)} custom-call(f32[3456,128]{1,0:T(8,128)} %bitcast.13, f32[3456,128]{1,0:T(8,128)} %bitcast.16), custom_call_target="tpu_custom_call" | custom-call | tf_op jit(solution)/shard_map/pallas_call | solution.py:414
  167.9 4.0 %fusion = (f32[3456,128]{1,0:T(8,128)}, f32[3456,128]{1,0:T(8,128)}) fusion(f32[6912,128]{1,0:T(8,128)} %shard_map.81), kind=kLoop, calls=%fused_computation.1 | loop fusion | bytes 7077888 | tf_op jit(solution)/shard_map/slice | solution.py:424
Async XLA Ops:
  60.0 9.2 %copy-start = (bf16[27,128,128]{2,1,0:T(8,128)(2,1)S(1)}, bf16[27,128,128]{2,1,0:T(8,128)(2,1)}, u32[]{:S(2)}) copy-start(bf16[27,128,128]{2,1,0:T(8,128)(2,1)} %param.7) | copy-start | bytes 2654212

commit v3 on v2

--- a/solution.py
+++ b/solution.py
@@ -32,10 +32,10 @@
     return {0: 0, 7: 64}.get(plane, 128 + 32 * (plane - 1))
 
 
-def pack_shell(block, own_ref, shell_ref, base=0):
+def pack_shell(block, own_ref, shell_ref):
     channels = own_ref.shape[-1]
     for plane in (0, 7):
-        shell_ref[block, pl.ds(base + plane_start(plane), 64), :] = own_ref[block, plane]
+        shell_ref[block, pl.ds(plane_start(plane), 64), :] = own_ref[block, plane]
     for plane in range(1, 7):
         lines = lines_of(own_ref[block, plane])
         cell = lax.broadcasted_iota(jnp.int32, (1, 8, channels), 1)
@@ -48,17 +48,17 @@
             ends.append(packed)
         packed = jnp.concatenate([lines[0:1], lines[7:8]] + ends, axis=0)
         packed = packed.reshape(32, channels).astype(jnp.bfloat16)
-        shell_ref[block, pl.ds(base + plane_start(plane), 32), :] = packed
-
-
-def build_slab(block, own_ref, table_ref, place_ref, pad_ref, slab_ref, base=0):
+        shell_ref[block, pl.ds(plane_start(plane), 32), :] = packed
+
+
+def build_slab(block, own_ref, table_ref, place_ref, pad_ref, slab_ref):
     channels = own_ref.shape[-1]
 
     def source(step_x, step_y, step_z, plane):
         if (step_x, step_y, step_z) == (0, 0, 0):
             return lines_of(own_ref[block, plane])
         where = place_ref[block, offset_index(step_x, step_y, step_z)]
-        near, start = jnp.maximum(where, 0), base + plane_start(plane)
+        near, start = jnp.maximum(where, 0), plane_start(plane)
         if plane in (0, 7):
             if step_y == 0:
                 got = lines_of(table_ref[near, pl.ds(start, 64), :])
@@ -149,35 +149,86 @@
     return 1.0 / (1.0 + jnp.exp(-values))
 
 
-def pack_kernel(own_ref, cot_ref, shell_ref):
+def pack_all(field_ref, shell_ref):
     def step(block, carry):
-        pack_shell(block, own_ref, shell_ref)
-        pack_shell(block, cot_ref, shell_ref, SHELL)
+        pack_shell(block, field_ref, shell_ref)
         return carry
 
-    lax.fori_loop(0, own_ref.shape[0], step, 0)
-
-
-def first_kernel(
-    place_ref, own_ref, table_ref, weight_ref, pre_ref, hidden_ref, shell_ref, pad_ref, slab_ref
-):
+    lax.fori_loop(0, field_ref.shape[0], step, 0)
+
+
+def flip_taps(weight_ref, flipped_ref):
+    taps = weight_ref.shape[0]
+    for tap in range(taps):
+        flipped_ref[tap] = weight_ref[taps - 1 - tap].T
+
+
+def pack_kernel(own_ref, cot_ref, weight_ref, shell_ref, cot_shell_ref, flipped_ref):
+    pack_all(own_ref, shell_ref)
+    pack_all(cot_ref, cot_shell_ref)
+    flip_taps(weight_ref, flipped_ref)
+
+
+def pack_ring_kernel(
+    devices, own_ref, cot_ref, weight_ref, table_ref, cot_shell_ref, flipped_ref, shell_ref, *sems
+):
+    pack_all(own_ref, shell_ref)
+    begin, advance, finish = ring(devices, shell_ref, table_ref, *sems)
+    begin()
+    pack_all(cot_ref, cot_shell_ref)
+    flip_taps(weight_ref, flipped_ref)
+    for step in range(devices - 1):
+        advance(step, step == devices - 2)
+    finish()
+
+
+def first_step(
+    block, place_ref, own_ref, table_ref, weight_ref, pre_ref, hidden_ref, shell_ref,
+    pad_ref, slab_ref,
+):
+    build_slab(block, own_ref, table_ref, place_ref, pad_ref, slab_ref)
+    pre = conv_slab(slab_ref, weight_ref)
+    pre_ref[block] = pre
+    hidden = (pre / (1.0 + jnp.exp(-pre))).astype(jnp.bfloat16)
+    hidden_ref[block] = hidden.reshape(hidden_ref.shape[1:])
+    pack_shell(block, hidden_ref, shell_ref)
+
+
+def first_kernel(*refs):
     def step(block, carry):
-        build_slab(block, own_ref, table_ref, place_ref, pad_ref, slab_ref)
-        pre = conv_slab(slab_ref, weight_ref)
-        pre_ref[block] = pre
-        hidden = (pre / (1.0 + jnp.exp(-pre))).astype(jnp.bfloat16)
-        hidden_ref[block] = hidden.reshape(hidden_ref.shape[1:])
-        pack_shell(block, hidden_ref, shell_ref)
+        first_step(block, *refs)
         return carry
 
-    lax.fori_loop(0, own_ref.shape[0], step, 0)
+    lax.fori_loop(0, refs[1].shape[0], step, 0)
+
+
+def first_ring_kernel(
+    devices, place_ref, own_ref, table_ref, weight_ref, payload_ref,
+    pre_ref, hidden_ref, shell_ref, cot_table_ref, pad_ref, slab_ref, *sems,
+):
+    begin, advance, finish = ring(devices, payload_ref, cot_table_ref, *sems)
+    begin()
+    count = own_ref.shape[0]
+
+    def step(block, carry):
+        first_step(
+            block, place_ref, own_ref, table_ref, weight_ref, pre_ref, hidden_ref, shell_ref,
+            pad_ref, slab_ref,
+        )
+        advance(block, False)
+        return carry
+
+    lax.fori_loop(0, count, step, 0)
+    for later in range(count, devices - 1):
+        advance(later, later == devices - 2)
+    finish()
 
 
 def back_step(
-    block, place_ref, own_ref, table_ref, cot_ref, weight_ref, pre_ref,
+    block, place_ref, own_ref, table_ref, cot_ref, cot_table_ref, weight_ref, pre_ref,
     pad_ref, slab_ref, spread_ref, total_ref,
 ):
-    build_slab(block, cot_ref, table_ref, place_ref, pad_ref, slab_ref, SHELL)
+    build_slab(block, cot_ref, cot_table_ref, place_ref, pad_ref, slab_ref)
     back = conv_slab(slab_ref, weight_ref)
     pre = pre_ref[block]
     sig = sigmoid(pre)
@@ -187,13 +238,17 @@
     add_taps(total_ref, spread_ref, slab_ref)
 
 
-def back_kernel(scale, place_ref, own_ref, table_ref, cot_ref, weight_ref, pre_ref, grad_ref, *scratch):
+def back_kernel(
+    scale, place_ref, own_ref, table_ref, cot_ref, cot_table_ref, weight_ref, pre_ref, grad_ref,
+    *scratch,
+):
     total_ref = scratch[-1]
     total_ref[...] = jnp.zeros_like(total_ref)
 
     def step(block, carry):
         back_step(
-            block, place_ref, own_ref, table_ref, cot_ref, weight_ref, pre_ref, *scratch
+            block, place_ref, own_ref, table_ref, cot_ref, cot_table_ref, weight_ref, pre_ref,
+            *scratch,
         )
         return carry
 
@@ -202,7 +257,8 @@
 
 
 def back_ring_kernel(
-    scale, devices, place_ref, own_ref, table_ref, cot_ref, weight_ref, pre_ref, payload_ref,
+    scale, devices, place_ref, own_ref, table_ref, cot_ref, cot_table_ref, weight_ref, pre_ref,
+    payload_ref,
     grad_ref, hidden_table_ref, pad_ref, slab_ref, spread_ref, total_ref, *sems,
 ):
     begin, advance, finish = ring(devices, payload_ref, hidden_table_ref, *sems)
@@ -212,7 +268,7 @@
 
     def step(block, carry):
         back_step(
-            block, place_ref, own_ref, table_ref, cot_ref, weight_ref, pre_ref,
+            block, place_ref, own_ref, table_ref, cot_ref, cot_table_ref, weight_ref, pre_ref,
             pad_ref, slab_ref, spread_ref, total_ref,
         )
         advance(block, False)
@@ -297,14 +353,6 @@
         own.wait()
 
     return begin, advance, finish
-
-
-def ring_kernel(devices, payload_ref, table_ref, *sems):
-    begin, advance, finish = ring(devices, payload_ref, table_ref, *sems)
-    begin()
-    for step in range(devices - 1):
-        advance(step, step == devices - 2)
-    finish()
 
 
 def ring_sems(devices, count):
@@ -461,16 +509,9 @@
         gap = links // block_count - lax.axis_index("blocks")
         placed = jnp.where(links >= 0, (gap + reach) * block_count + links % block_count, -1)
 
-    ringed = whole and devices % 2 == 0 and block_count % 2 == 0
-
-    def collect(payload, collective_id):
-        if ringed:
-            (table,) = call(
-                functools.partial(ring_kernel, devices),
-                [ring_table(payload, devices)], ring_sems(devices, block_count), 0, payload,
-                collective_id=collective_id, has_side_effects=True,
-            )
-            return table
+    ringed = whole and devices % 2 == 0 and block_count % 2 == 0 and block_count < devices - 1
+
+    def collect(payload):
         if whole:
             return lax.all_gather(payload, "blocks", axis=0, tiled=True)
         pieces = [
@@ -482,7 +523,6 @@
     def slabs(weights):
         return weights.reshape(3, 9 * channels, channels)
 
-    flipped = jnp.transpose(weight_two[::-1], (0, 2, 1))
     voxels = lax.axis_size("rep") * devices * block_count * 512
     scale = 1.0 / math.sqrt(voxels)
     flops = 2 * block_count * 512 * 27 * channels * channels
@@ -495,30 +535,43 @@
     grads = jax.ShapeDtypeStruct(weight_one.shape, f32)
 
     shell = jax.ShapeDtypeStruct((block_count, SHELL, channels), bf16)
-    both = jax.ShapeDtypeStruct((block_count, 2 * SHELL, channels), bf16)
-
-    (shells,) = call(pack_kernel, [both], [], 0, own, cot)
-    table = collect(shells, 1)
-    pre, hidden, hidden_shell = call(
-        first_kernel,
-        [jax.ShapeDtypeStruct(rows, f32), jax.ShapeDtypeStruct(own.shape, bf16), shell],
-        [pad, slab], flops,
-        placed, own, table, slabs(weight_one),
-    )
-    back_operands = (placed, own, table, cot, slabs(flipped), pre)
+    flipped_taps = jax.ShapeDtypeStruct(weight_two.shape, bf16)
+    pre_and_hidden = [
+        jax.ShapeDtypeStruct(rows, f32), jax.ShapeDtypeStruct(own.shape, bf16), shell
+    ]
     back_scratch = [pad, slab, spread, total]
-    if ringed and block_count < devices - 1:
+    if ringed:
+        gathered, sems = ring_table(shell, devices), ring_sems(devices, block_count)
+        table, cot_shell, flipped = call(
+            functools.partial(pack_ring_kernel, devices), [gathered, shell, flipped_taps],
+            [pltpu.VMEM(shell.shape, bf16)] + sems, 0, own, cot, weight_two,
+            collective_id=1, has_side_effects=True,
+        )
+        pre, hidden, hidden_shell, cot_table = call(
+            functools.partial(first_ring_kernel, devices), pre_and_hidden + [gathered],
+            [pad, slab] + sems, flops,
+            placed, own, table, slabs(weight_one), cot_shell,
+            collective_id=2, has_side_effects=True,
+        )
         grad_one, hidden_table = call(
-            functools.partial(back_ring_kernel, scale, devices),
-            [grads, ring_table(hidden_shell, devices)],
-            back_scratch + ring_sems(devices, block_count), 2 * flops,
-            *back_operands, hidden_shell,
-            collective_id=2, has_side_effects=True,
+            functools.partial(back_ring_kernel, scale, devices), [grads, gathered],
+            back_scratch + sems, 2 * flops,
+            placed, own, table, cot, cot_table, slabs(flipped), pre, hidden_shell,
+            collective_id=3, has_side_effects=True,
         )
     else:
-        hidden_table = collect(hidden_shell, 2)
+        own_shell, cot_shell, flipped = call(
+            pack_kernel, [shell, shell, flipped_taps], [], 0, own, cot, weight_two
+        )
+        table, cot_table = collect(own_shell), collect(cot_shell)
+        pre, hidden, hidden_shell = call(
+            first_kernel, pre_and_hidden, [pad, slab], flops,
+            placed, own, table, slabs(weight_one),
+        )
+        hidden_table = collect(hidden_shell)
         (grad_one,) = call(
-            functools.partial(back_kernel, scale), [grads], back_scratch, 2 * flops, *back_operands
+            functools.partial(back_kernel, scale), [grads], back_scratch, 2 * flops,
+            placed, own, table, cot, cot_table, slabs(flipped), pre,
         )
     out, grad_two = call(
         functools.partial(second_kernel, scale),
@@ -527,7 +580,7 @@
     )
     counts = (devices, lax.axis_size("rep"))
     if can_halve(counts, 2 * grad_one.size // channels):
-        grad_one, grad_two = sum_everywhere(grad_one, grad_two, *counts, 3)
+        grad_one, grad_two = sum_everywhere(grad_one, grad_two, *counts, 4)
     else:
         grad_one, grad_two = lax.psum((grad_one, grad_two), ("blocks", "rep"))
     return out.reshape(features.shape), grad_one, grad_two

time: 172 us -> 168 us (0.977)
  Pallas kernels: 165 us -> 163 us
  local copies, waits for them, and re-layouts: 5.76 us -> 4.03 us
    pallas_call x5 -> x4, Pallas kernels: 114 us -> 109 us  [call(): pl.pallas_call(body, out_shape=outs, in_specs=specs, out_specs=[space] *...]
    pallas_call x1, Pallas kernels: 51.3 us -> 53.7 us  [sum_everywhere(): pl.pallas_call(functools.partial(sum_kernel, orders), out_shape=jax.Shape...]
    transpose x2 -> x0, local copies, waits for them, and re-layouts: 1.72 us -> none  [local(): flipped = jnp.transpose(weight_two[::-1], (0, 2, 1))]
where the time goes in v3:
time: 168 us; the launch traced here: 167 us
  Pallas kernels  163 us (97%)
  local copies, waits for them, and re-layouts  4.03 us (2%)
    pallas_call x4, Pallas kernels, call(): pl.pallas_call(body, out_shape=outs, in_specs=specs, out_specs=[space] *...  109 us
    pallas_call x1, Pallas kernels, sum_everywhere(): pl.pallas_call(functools.partial(sum_kernel, orders), out_shape=jax.Shape...  53.7 us
    slice x1, local copies, waits for them, and re-layouts, sum_everywhere(): out[rows // 2:].reshape(two.shape)  4.03 us

profile of v3, /device:TPU:1, one launch (start us, length us, event | category | flops | bytes accessed | tf_op | source)
XLA Modules:
  0.0 167.3 jit_solution(3931280946352219608)
XLA Ops:
  0.6 32.2 %shard_map.76 = (bf16[32,320,128]{2,1,0:T(8,128)(2,1)}, bf16[4,320,128]{2,1,0:T(8,128)(2,1)}, bf16[27,128,128]{2,1,0:T(8,128)(2,1)}) custom-call(bf16[4,8,64,128]{3,2,1,0:T(8,128)(2,1)} %bitcast.16, bf16[4,8,64,128]{3,2,1,0:T(8,128)(2,1)} %bitcast.19, bf16[27,128,128]{2,1,0:T(8,128)(2,1)} %weight_ref.1), custom_call_target="tpu_custom_call" | custom-call | bytes 1933312 | tf_op jit(solution)/shard_map/pallas_call | solution.py:487
  32.8 31.4 %shard_map.77 = (f32[4,512,128]{2,1,0:T(8,128)}, bf16[4,8,64,128]{3,2,1,0:T(8,128)(2,1)}, bf16[4,320,128]{2,1,0:T(8,128)(2,1)}, bf16[32,320,128]{2,1,0:T(8,128)(2,1)}) custom-call(s32[4,26]{1,0:T(4,128)} %bitcast.24, bf16[4,8,64,128]{3,2,1,0:T(8,128)(2,1)} %bitcast.17, bf16[32,320,128]{2,1,0:T(8,128)(2,1)} %get-tuple-element.14.table_ref, ...), custom_call_target="tpu_custom_call" | custom-call | flops 1811939328 | bytes 4358560 | tf_op jit(solution)/shard_map/pallas_call | solution.py:487
  64.3 33.2 %shard_map.78 = (f32[27,128,128]{2,1,0:T(8,128)}, bf16[32,320,128]{2,1,0:T(8,128)(2,1)}) custom-call(s32[4,26]{1,0:T(4,128)} %bitcast.25, bf16[4,8,64,128]{3,2,1,0:T(8,128)(2,1)} %bitcast.18, bf16[32,320,128]{2,1,0:T(8,128)(2,1)} %get-tuple-element.14.table_ref, bf16[4,8,64,128]{3,2,1,0:T(8,128)(2,1)} %bitcast.20, ...), custom_call_target="tpu_custom_call" | custom-call | flops 3623878656 | bytes 8552864 | tf_op jit(solution)/shard_map/pallas_call | solution.py:487
  97.5 12.1 %shard_map.79 = (bf16[4,512,128]{2,1,0:T(8,128)(2,1)}, f32[27,128,128]{2,1,0:T(8,128)}) custom-call(s32[4,26]{1,0:T(4,128)} %bitcast.26, bf16[4,8,64,128]{3,2,1,0:T(8,128)(2,1)} %get-tuple-element.16.own_ref, bf16[32,320,128]{2,1,0:T(8,128)(2,1)} %get-tuple-element.21.table_ref, bf16[4,8,64,128]{3,2,1,0:T(8,128)(2,1)} %bitcast.21, bf16[3,1152,128]{2,1,0:T(8,128)(2,1)} %bitcast.15), custom_call_target="tpu_custom_call" | custom-call | flops 3623878656 | bytes 4555168 | tf_op jit(solution)/shard_map/pallas_call | solution.py:487
  109.6 53.7 %shard_map.80 = f32[6912,128]{1,0:T(8,128)} custom-call(f32[3456,128]{1,0:T(8,128)} %bitcast.11, f32[3456,128]{1,0:T(8,128)} %bitcast.14), custom_call_target="tpu_custom_call" | custom-call | tf_op jit(solution)/shard_map/pallas_call | solution.py:462
  163.3 4.0 %fusion = (f32[3456,128]{1,0:T(8,128)}, f32[3456,128]{1,0:T(8,128)}) fusion(f32[6912,128]{1,0:T(8,128)} %shard_map.80), kind=kLoop, calls=%fused_computation | loop fusion | bytes 7077888 | tf_op jit(solution)/shard_map/slice | solution.py:472

commit v4 on v3

--- a/solution.py
+++ b/solution.py
@@ -396,8 +396,14 @@
             barrier, inc=1, device_id=partner(dim), device_id_type=pl.DeviceIdType.MESH
         )
     pl.semaphore_wait(barrier, levels)
-    held_ref[pl.ds(0, rows // 2), :] = one_ref[...]
-    held_ref[pl.ds(rows // 2, rows // 2), :] = two_ref[...]
+
+    def load(low, high):
+        for source_ref, base in ((one_ref, 0), (two_ref, rows // 2)):
+            first, end = max(low, base), min(high, base + rows // 2)
+            if first < end:
+                held_ref[pl.ds(first, end - first), :] = source_ref[
+                    pl.ds(first - base, end - first), :
+                ]
 
     def copy_to(part, step, dim, source, target):
         return pltpu.make_async_remote_copy(
@@ -415,7 +421,9 @@
     for step in range(levels + 1):
         for part, order in enumerate(orders):
             half = shares[part] >> (step + 1)
-            if step:
+            if step == 0:
+                load(cuts[part], cuts[part + 1])
+            else:
                 flying[part].wait_recv()
                 size = shares[part] >> step
                 mine = pl.ds(pl.multiple_of(starts[part][-1], 8), size)

time: 168 us -> 167 us (level)
  no operation moved by 1% of the time
where the time goes in v4:
time: 167 us
  Pallas kernels  162 us (97%)
  local copies, waits for them, and re-layouts  4.03 us (2%)
    pallas_call x4, Pallas kernels, call(): pl.pallas_call(body, out_shape=outs, in_specs=specs, out_specs=[space] *...  109 us
    pallas_call x1, Pallas kernels, sum_everywhere(): pl.pallas_call(functools.partial(sum_kernel, orders), out_shape=jax.Shape...  53.4 us
    slice x1, local copies, waits for them, and re-layouts, sum_everywhere(): out[rows // 2:].reshape(two.shape)  4.03 us

profile of v4, /device:TPU:1, one launch (start us, length us, event | category | flops | bytes accessed | tf_op | source)
XLA Modules:
  0.0 167.0 jit_solution(4152625736053891818)
XLA Ops:
  0.6 32.2 %shard_map.76 = (bf16[32,320,128]{2,1,0:T(8,128)(2,1)}, bf16[4,320,128]{2,1,0:T(8,128)(2,1)}, bf16[27,128,128]{2,1,0:T(8,128)(2,1)}) custom-call(bf16[4,8,64,128]{3,2,1,0:T(8,128)(2,1)} %bitcast.16, bf16[4,8,64,128]{3,2,1,0:T(8,128)(2,1)} %bitcast.19, bf16[27,128,128]{2,1,0:T(8,128)(2,1)} %weight_ref.1), custom_call_target="tpu_custom_call" | custom-call | bytes 1933312 | tf_op jit(solution)/shard_map/pallas_call | solution.py:495
  32.8 31.4 %shard_map.77 = (f32[4,512,128]{2,1,0:T(8,128)}, bf16[4,8,64,128]{3,2,1,0:T(8,128)(2,1)}, bf16[4,320,128]{2,1,0:T(8,128)(2,1)}, bf16[32,320,128]{2,1,0:T(8,128)(2,1)}) custom-call(s32[4,26]{1,0:T(4,128)} %bitcast.24, bf16[4,8,64,128]{3,2,1,0:T(8,128)(2,1)} %bitcast.17, bf16[32,320,128]{2,1,0:T(8,128)(2,1)} %get-tuple-element.14.table_ref, ...), custom_call_target="tpu_custom_call" | custom-call | flops 1811939328 | bytes 4358560 | tf_op jit(solution)/shard_map/pallas_call | solution.py:495
  64.3 33.2 %shard_map.78 = (f32[27,128,128]{2,1,0:T(8,128)}, bf16[32,320,128]{2,1,0:T(8,128)(2,1)}) custom-call(s32[4,26]{1,0:T(4,128)} %bitcast.25, bf16[4,8,64,128]{3,2,1,0:T(8,128)(2,1)} %bitcast.18, bf16[32,320,128]{2,1,0:T(8,128)(2,1)} %get-tuple-element.14.table_ref, bf16[4,8,64,128]{3,2,1,0:T(8,128)(2,1)} %bitcast.20, ...), custom_call_target="tpu_custom_call" | custom-call | flops 3623878656 | bytes 8552864 | tf_op jit(solution)/shard_map/pallas_call | solution.py:495
  97.5 12.1 %shard_map.79 = (bf16[4,512,128]{2,1,0:T(8,128)(2,1)}, f32[27,128,128]{2,1,0:T(8,128)}) custom-call(s32[4,26]{1,0:T(4,128)} %bitcast.26, bf16[4,8,64,128]{3,2,1,0:T(8,128)(2,1)} %get-tuple-element.16.own_ref, bf16[32,320,128]{2,1,0:T(8,128)(2,1)} %get-tuple-element.21.table_ref, bf16[4,8,64,128]{3,2,1,0:T(8,128)(2,1)} %bitcast.21, bf16[3,1152,128]{2,1,0:T(8,128)(2,1)} %bitcast.15), custom_call_target="tpu_custom_call" | custom-call | flops 3623878656 | bytes 4555168 | tf_op jit(solution)/shard_map/pallas_call | solution.py:495
  109.6 53.4 %shard_map.80 = f32[6912,128]{1,0:T(8,128)} custom-call(f32[3456,128]{1,0:T(8,128)} %bitcast.11, f32[3456,128]{1,0:T(8,128)} %bitcast.14), custom_call_target="tpu_custom_call" | custom-call | tf_op jit(solution)/shard_map/pallas_call | solution.py:470
  163.0 4.0 %fusion = (f32[3456,128]{1,0:T(8,128)}, f32[3456,128]{1,0:T(8,128)}) fusion(f32[6912,128]{1,0:T(8,128)} %shard_map.80), kind=kLoop, calls=%fused_computation | loop fusion | bytes 7077888 | tf_op jit(solution)/shard_map/slice | solution.py:480
